TPU v7x, 512 devices: a whole 4x4x16 slice. The times are simulated.
512 devices in a mesh: group: 8 (over x, core), dev: 64 (over z, y).
Axes of the slice: x: 4, y: 4, z: 16, core: 2. Of those that a mesh axis runs over, the one named last changes fastest.
Arguments:
- cam_jac: float32 [2, 9, 8, 262144], P(None, None, None, ('group', 'dev')), may hold values from -6 to 6
- lm_jac: float32 [2, 3, 8, 262144], P(None, None, None, ('group', 'dev')), may hold values from -6 to 6
- resid: float32 [2, 8, 262144], P(None, None, ('group', 'dev')), may hold values from -6 to 6
- cam_index: int32 [8, 262144], P(None, ('group', 'dev')), may hold values from 0 to 8191
Outputs:
- camera_step: float32 [9, 8192], P(None, 'dev')
- camera_residual: float32 [9, 8192], P(None, 'dev')
- landmark_step: float32 [3, 262144], P(None, ('group', 'dev'))
Inputs may be any that keep to these rules, and one draw needn't show every extreme that they name: `cam_index`: every observation names one of the 8192 cameras.
All inputs are finite; a program needn't handle non-finite values.
Results may differ from a plain program's by a relative error of at most 0.0003.
Values sent between devices are 32-bit elements; how exact they have to be, the bound alone decides.
A program may use at most 64 MiB of HBM per device.

v0:
```python
import jax
import jax.numpy as jnp
from jax import lax
from jax.sharding import PartitionSpec as P

CAM_DEV = 128
ITERS = 2
DAMPING = 1.0


def landmark_inverse(lm_jac):

    def entry(first, second):
        return jnp.sum(lm_jac[:, first] * lm_jac[:, second], axis=(0, 1))

    w_00 = entry(0, 0) + DAMPING
    w_11 = entry(1, 1) + DAMPING
    w_22 = entry(2, 2) + DAMPING
    w_01 = entry(0, 1)
    w_02 = entry(0, 2)
    w_12 = entry(1, 2)
    cof_00 = w_11 * w_22 - w_12 * w_12
    cof_01 = w_02 * w_12 - w_01 * w_22
    cof_02 = w_01 * w_12 - w_02 * w_11
    cof_11 = w_00 * w_22 - w_02 * w_02
    cof_12 = w_01 * w_02 - w_00 * w_12
    cof_22 = w_00 * w_11 - w_01 * w_01
    determinant = w_00 * cof_00 + w_01 * cof_01 + w_02 * cof_02
    rows = [
        jnp.stack([cof_00, cof_01, cof_02]),
        jnp.stack([cof_01, cof_11, cof_12]),
        jnp.stack([cof_02, cof_12, cof_22]),
    ]
    return jnp.stack(rows) / determinant[None, None]


def apply_inverse(inverse, vector):
    return jnp.sum(inverse * vector[None], axis=1)


def landmark_side(lm_jac, values):
    return jnp.sum(lm_jac * values[:, None], axis=(0, 2))


def back_project(lm_jac, landmark):
    return jnp.sum(lm_jac * landmark[None, :, None, :], axis=1)


def camera_apply(cam_jac, cam_values):
    return jnp.sum(cam_jac * cam_values[None], axis=1)


def camera_transpose(cam_jac, errors):
    return jnp.sum(cam_jac * errors[:, None], axis=0)


def to_cameras(values, cam_index, total_cams):
    flat_index = cam_index.reshape(-1)
    width = values.shape[0]

    def one_row(column):
        return jax.ops.segment_sum(column, flat_index, num_segments=total_cams)

    return jax.vmap(one_row)(values.reshape(width, -1))


def schur_obs(cam_jac, lm_jac, inverse, cam_values):
    applied = camera_apply(cam_jac, cam_values)
    landmark = apply_inverse(inverse, landmark_side(lm_jac, applied))
    return camera_transpose(cam_jac, applied - back_project(lm_jac, landmark))


def gather_cameras(tile):
    return lax.all_gather(tile, "dev", axis=1, tiled=True)


def reduce_cameras(terms):
    totals = lax.psum(terms, ("group", "dev"))
    width = terms.shape[1] // lax.axis_size("dev")
    return lax.dynamic_slice_in_dim(totals, lax.axis_index("dev") * width, width, 1)


def inner_product(left, right):
    return lax.psum(jnp.sum(left * right), "dev")


def body(cam_jac, lm_jac, resid, cam_index):
    total_cams = CAM_DEV * lax.axis_size("dev")
    inverse = landmark_inverse(lm_jac)
    land_rhs = apply_inverse(inverse, landmark_side(lm_jac, resid))
    errors = resid - back_project(lm_jac, land_rhs)
    stacked = jnp.concatenate(
        [camera_transpose(cam_jac, errors), jnp.sum(cam_jac * cam_jac, axis=0)], axis=0
    )
    summed = reduce_cameras(to_cameras(stacked, cam_index, total_cams))
    gradient = summed[:9]
    diagonal = summed[9:] + DAMPING
    residual = gradient
    precond = residual / diagonal
    direction = precond
    rz_now = inner_product(residual, precond)
    solution = jnp.zeros_like(gradient)
    for iteration in range(ITERS):
        whole = gather_cameras(direction)
        cam_values = jnp.take(whole, cam_index, axis=1)
        terms = to_cameras(schur_obs(cam_jac, lm_jac, inverse, cam_values), cam_index, total_cams)
        image = reduce_cameras(terms) + DAMPING * direction
        alpha = rz_now / inner_product(direction, image)
        solution = solution + alpha * direction
        residual = residual - alpha * image
        if iteration + 1 < ITERS:
            precond = residual / diagonal
            rz_next = inner_product(residual, precond)
            direction = precond + rz_next / rz_now * direction
            rz_now = rz_next
    whole_step = gather_cameras(solution)
    cam_obs = camera_apply(cam_jac, jnp.take(whole_step, cam_index, axis=1))
    landmark_step = land_rhs - apply_inverse(inverse, landmark_side(lm_jac, cam_obs))
    return (solution, residual, landmark_step)


def solution(mesh):
    in_specs = (
        P(None, None, None, ("group", "dev")),
        P(None, None, None, ("group", "dev")),
        P(None, None, ("group", "dev")),
        P(None, ("group", "dev")),
    )
    out_specs = (P(None, "dev"), P(None, "dev"), P(None, ("group", "dev")))
    return jax.shard_map(body, mesh=mesh, in_specs=in_specs, out_specs=out_specs, check_vma=False)
```

profile of v0, /device:TPU:8, one launch (start us, length us, event | category | flops | bytes accessed | tf_op | source)
XLA Modules:
  0.0 2390.0 jit_solution(14837299796872105308)
XLA Ops:
  7.2 0.0 all-reduce.5.cloned.1.call-start
  7.2 0.8 multiply_reduce_fusion.22
  8.0 0.9 multiply_reduce_fusion.13
  9.0 0.7 copy.31
  9.8 0.9 multiply_reduce_fusion.12
  10.7 0.8 sub.128
  11.5 1.0 multiply_reduce_fusion.6
  12.5 0.6 copy.28
  13.2 0.0 copy-start.2
  13.2 24.5 %scatter_custom_fusion = f32[18,8192]{0,1:T(8,128)} fusion(s32[4096]{0:T(1024)S(1)} %bitcast.43, f32[4096,18]{1,0:T(8,128)S(1)} %bitcast.38, f32[]{:T(128)} %constant.14.clone.1), kind=kCustom, calls=%fused_computation.13 | custom fusion | flops 73728 | bytes 589828 | tf_op jit(solution)/shard_map/vmap()/scatter-add | solution.py:62
  37.7 0.0 all-reduce.5.cloned.1.call-update
  37.8 0.0 all-reduce.7.cloned.1.call-start
  37.8 0.0 copy-done.2
  37.9 494.2 %all-reduce.5.cloned.1.call-done = f32[18,8192]{0,1:T(8,128)} async-done(((f32[18,8192]{0,1:T(8,128)}), f32[18,8192]{0,1:T(8,128)}) %all-reduce.5.cloned.1.call-update) | async-done | bytes 589840 | tf_op jit(solution)/shard_map/psum | solution.py:78
  532.1 1.0 fusion.7
  533.1 111.9 %all_gather.9 = f32[9,8192]{0,1:T(8,128)} all-gather(f32[9,128]{0,1:T(8,128)S(1)} %fusion.7), channel_id=1, replica_groups=mesh['group'=8,'dev'=64] {'dev'}, dimensions={1}, use_global_device_ids=true | all-gather | bytes 299520 | tf_op jit(solution)/shard_map/all_gather | solution.py:74
  645.0 0.0 copy-start
  645.0 0.0 copy-start.1
  645.0 16.3 gather_fusion
  661.3 1.9 select_bitcast_fusion.2
  663.3 0.6 copy.21
  663.9 0.0 copy-done
  664.0 0.0 copy-done.1
  664.1 0.6 copy.29
  664.8 24.5 %scatter_custom_fusion.1 = f32[9,8192]{0,1:T(8,128)} fusion(s32[4096]{0:T(1024)S(1)} %bitcast.44, f32[4096,9]{1,0:T(8,128)S(1)} %bitcast.40, f32[]{:T(128)} %constant.14.clone.1), kind=kCustom, calls=%fused_computation.11 | custom fusion | flops 36864 | bytes 294916 | tf_op jit(solution)/shard_map/vmap()/scatter-add | solution.py:62
  689.3 0.0 all-reduce.7.cloned.1.call-update
  689.3 0.0 all-reduce.9.cloned.1.call-start
  689.4 488.0 %all-reduce.7.cloned.1.call-done = f32[9,8192]{0,1:T(8,128)} async-done(((f32[9,8192]{0,1:T(8,128)}), f32[9,8192]{0,1:T(8,128)}) %all-reduce.7.cloned.1.call-update) | async-done | bytes 294928 | tf_op jit(solution)/shard_map/psum | solution.py:78
  1177.4 1.6 multiply_reduce_fusion.16
  1179.0 139.5 %all-reduce = (f32[]{:T(128)}, f32[]{:T(128)}) all-reduce(f32[]{:T(128)} %get-tuple-element.22, f32[]{:T(128)} %get-tuple-element.21), channel_id=1, replica_groups=mesh['group'=8,'dev'=64] {'dev'}, use_global_device_ids=true, to_apply=%region_14.0 | all-reduce | flops 2 | bytes 16 | tf_op jit(solution)/shard_map/psum | solution.py:84
  1319.8 1.6 multiply_reduce_fusion.15
  1321.4 140.7 %psum.53 = f32[]{:T(128)} all-reduce(f32[]{:T(128)} %get-tuple-element.25), channel_id=1, replica_groups=mesh['group'=8,'dev'=64] {'dev'}, use_global_device_ids=true, to_apply=%region_25.27 | all-reduce | flops 1 | bytes 8 | tf_op jit(solution)/shard_map/psum | solution.py:84
  1463.5 1.0 multiply_add_fusion.1
  1464.5 110.5 %all_gather.10 = f32[9,8192]{0,1:T(8,128)} all-gather(f32[9,128]{0,1:T(8,128)S(1)} %multiply_add_fusion.1), channel_id=1, replica_groups=mesh['group'=8,'dev'=64] {'dev'}, dimensions={1}, use_global_device_ids=true | all-gather | bytes 299520 | tf_op jit(solution)/shard_map/all_gather | solution.py:74
  1575.0 16.3 gather_fusion.1
  1591.2 1.9 select_bitcast_fusion.1
  1593.2 0.6 copy.23
  1594.0 0.6 copy.30
  1594.6 24.5 %scatter_custom_fusion.2 = f32[9,8192]{0,1:T(8,128)} fusion(s32[4096]{0:T(1024)S(1)} %bitcast.45, f32[4096,9]{1,0:T(8,128)S(1)} %bitcast.39, f32[]{:T(128)} %constant.14.clone.1), kind=kCustom, calls=%fused_computation.9 | custom fusion | flops 36864 | bytes 294916 | tf_op jit(solution)/shard_map/vmap()/scatter-add | solution.py:62
  1619.2 0.0 all-reduce.9.cloned.1.call-update
  1619.2 488.2 %all-reduce.9.cloned.1.call-done = f32[9,8192]{0,1:T(8,128)} async-done(((f32[9,8192]{0,1:T(8,128)}), f32[9,8192]{0,1:T(8,128)}) %all-reduce.9.cloned.1.call-update) | async-done | bytes 294928 | tf_op jit(solution)/shard_map/psum | solution.py:78
  2107.4 1.5 multiply_reduce_fusion.14
  2108.9 139.4 %psum.55 = f32[]{:T(128)} all-reduce(f32[]{:T(128)} %multiply_reduce_fusion.14), channel_id=1, replica_groups=mesh['group'=8,'dev'=64] {'dev'}, use_global_device_ids=true, to_apply=%region_34.36 | all-reduce | flops 1 | bytes 8 | tf_op jit(solution)/shard_map/psum | solution.py:84
  2249.7 1.0 multiply_subtract_fusion
  2250.7 0.7 copy.26
  2251.4 111.8 %all_gather.11 = f32[9,8192]{0,1:T(8,128)} all-gather(f32[9,128]{0,1:T(8,128)S(1)} %get-tuple-element.34), channel_id=1, replica_groups=mesh['group'=8,'dev'=64] {'dev'}, dimensions={1}, use_global_device_ids=true | all-gather | bytes 299520 | tf_op jit(solution)/shard_map/all_gather | solution.py:74
  2363.2 0.7 copy.27
  2363.9 16.3 gather_fusion.2
  2380.2 1.9 select_bitcast_fusion
  2382.1 0.6 copy.25
  2382.8 0.6 sub.133
  (23 shorter events, 0.5 us)
Async XLA Ops:
  7.2 524.9 %all-reduce.5.cloned.1.call-start = ((), (), s32[]{:S(2)}) async-start(), calls=%async_computation | async-start | bytes 8388608 | tf_op jit(solution)/shard_map/psum | solution.py:78
  13.2 24.6 %copy-start.2 = (s32[8,512]{1,0:T(8,128)S(1)}, s32[8,512]{1,0:T(8,128)}, u32[]{:S(2)}) copy-start(s32[8,512]{1,0:T(8,128)} %param.9) | copy-start | bytes 49156
  37.8 1139.6 %all-reduce.7.cloned.1.call-start = ((), (), s32[]{:S(2)}) async-start(), calls=%async_computation.1 | async-start | bytes 8388608 | tf_op jit(solution)/shard_map/psum | solution.py:78
  645.0 18.9 copy-start
  645.0 19.0 copy-start.1
  689.3 1418.1 %all-reduce.9.cloned.1.call-start = ((), (), s32[]{:S(2)}) async-start(), calls=%async_computation.2 | async-start | bytes 8388608 | tf_op jit(solution)/shard_map/psum | solution.py:78
Sparse Core Ops, SparseCore 0:
  37.9 494.1 all-reduce.4
  689.4 487.8 all-reduce.6
  1619.3 488.0 all-reduce.8
where the time goes:
time: 2390 us
  waiting for transfers between devices  1470 us (62%)
  blocking collectives  754 us (32%)
  other arithmetic  92.8 us (4%)
  local copies, waits for them, and re-layouts  54.8 us (2%)
    psum x3, waiting for transfers between devices, reduce_cameras(): totals = lax.psum(terms, ('group', 'dev'))  1470 us
    psum x3, blocking collectives, inner_product(): return lax.psum(jnp.sum(left * right), 'dev')  420 us
    all_gather x3, blocking collectives, gather_cameras(): return lax.all_gather(tile, 'dev', axis=1, tiled=True)  334 us
    scatter-add x3, other arithmetic, one_row(): return jax.ops.segment_sum(column, flat_index, num_segments=total_cams)  73.6 us
  transfers between devices with their start and end apart: 3, of which 3 were waited for; matrix products, arithmetic and copies ran while one was open for 0% of the time, Pallas kernels for 0%

commit v1 on v0

--- a/solution.py
+++ b/solution.py
@@ -71,7 +71,13 @@
 
 
 def gather_cameras(tile):
-    return lax.all_gather(tile, "dev", axis=1, tiled=True)
+    bind_group = lambda piece_in, axis_id: jnp.concatenate(
+        lax.all_to_all(
+            jnp.stack([piece_in for _ in range(lax.axis_size(axis_id))], 0), axis_id, 0, 0
+        ),
+        1,
+    )
+    return bind_group(tile, axis_id="dev")
 
 
 def reduce_cameras(terms):

time: 2390 us -> 2090 us (0.87)
  the two profiles are of different devices: /device:TPU:8 before, /device:TPU:2 now
where the time goes in v1:
time: 2090 us
  waiting for transfers between devices  1410 us (67%)
  blocking collectives  489 us (23%)
  other arithmetic  92.2 us (4%)
  local copies, waits for them, and re-layouts  73.1 us (3%)
    psum x3, waiting for transfers between devices, reduce_cameras(): totals = lax.psum(terms, ('group', 'dev'))  1370 us
    psum x3, blocking collectives, inner_product(): return lax.psum(jnp.sum(left * right), 'dev')  426 us
    scatter-add x3, other arithmetic, one_row(): return jax.ops.segment_sum(column, flat_index, num_segments=total_cams)  73.5 us
    all_to_all x2, blocking collectives, gather_cameras(): lax.all_to_all(jnp.stack([piece_in for _ in range(lax.axis_size(axis_id))...  62.4 us
  transfers between devices with their start and end apart: 4, of which 4 were waited for; matrix products, arithmetic and copies ran while one was open for 0% of the time, Pallas kernels for 0%

profile of v1, /device:TPU:2, one launch (start us, length us, event | category | flops | bytes accessed | tf_op | source)
XLA Modules:
  0.0 2089.5 jit_solution(865818515667526034)
XLA Ops:
  7.2 0.0 all-reduce.5.cloned.1.call-start
  7.2 0.8 multiply_reduce_fusion.18
  8.0 0.9 multiply_reduce_fusion.13
  9.0 0.7 copy.55
  9.8 0.9 multiply_reduce_fusion.12
  10.7 0.8 sub.128
  11.5 1.0 multiply_reduce_fusion.6
  12.5 0.6 copy.52
  13.2 24.5 %scatter_custom_fusion = f32[18,8192]{0,1:T(8,128)} fusion(s32[4096]{0:T(1024)S(1)} %bitcast.55, f32[4096,18]{1,0:T(8,128)S(1)} %bitcast.50, f32[]{:T(128)} %constant.14.clone.1), kind=kCustom, calls=%fused_computation.13 | custom fusion | flops 73728 | bytes 589828 | tf_op jit(solution)/shard_map/vmap()/scatter-add | solution.py:62
  37.7 3.6 copy.41
  41.3 0.0 copy-start.2
  41.3 0.0 all-reduce.5.cloned.1.call-update
  41.3 473.1 %all-reduce.5.cloned.1.call-done = f32[18,8192]{1,0:T(8,128)} async-done(((f32[18,8192]{1,0:T(8,128)}), f32[18,8192]{1,0:T(8,128)}) %all-reduce.5.cloned.1.call-update) | async-done | bytes 589840 | tf_op jit(solution)/shard_map/psum | solution.py:84
  514.4 0.8 fusion.8
  515.3 0.8 stack.27
  516.1 12.2 all-to-all-start
  528.3 0.0 all-reduce.7.cloned.1.call-start
  528.4 0.0 copy-done.2
  528.4 31.9 %all-to-all-done = f32[64,9,128]{2,1,0:T(8,128)S(1)} async-done(((f32[64,9,128]{2,1,0:T(8,128)}), f32[64,9,128]{2,1,0:T(8,128)S(1)}, u32[]{:S(2)}, u32[]{:S(2)}) %all-to-all-start) | async-done | bytes 294944 | tf_op jit(solution)/shard_map/all_to_all | solution.py:75
  560.3 2.6 copy.42
  562.9 16.3 gather_fusion
  579.2 1.9 select_bitcast_fusion.2
  581.1 0.0 copy-start
  581.1 0.0 copy-start.1
  581.1 0.6 copy.43
  581.8 0.3 copy-done
  582.1 0.0 copy-done.1
  582.3 0.6 copy.53
  582.9 24.5 %scatter_custom_fusion.1 = f32[9,8192]{0,1:T(8,128)} fusion(s32[4096]{0:T(1024)S(1)} %bitcast.56, f32[4096,9]{1,0:T(8,128)S(1)} %bitcast.52, f32[]{:T(128)} %constant.14.clone.1), kind=kCustom, calls=%fused_computation.11 | custom fusion | flops 36864 | bytes 294916 | tf_op jit(solution)/shard_map/vmap()/scatter-add | solution.py:62
  607.4 3.5 copy.45
  611.0 0.0 all-reduce.7.cloned.1.call-update
  611.0 0.0 all-reduce.9.cloned.1.call-start
  611.0 450.9 %all-reduce.7.cloned.1.call-done = f32[9,8192]{1,0:T(8,128)} async-done(((f32[9,8192]{1,0:T(8,128)}), f32[9,8192]{1,0:T(8,128)}) %all-reduce.7.cloned.1.call-update) | async-done | bytes 294928 | tf_op jit(solution)/shard_map/psum | solution.py:84
  1062.0 1.5 multiply_reduce_fusion.26
  1063.4 141.3 %all-reduce = (f32[]{:T(128)}, f32[]{:T(128)}) all-reduce(f32[]{:T(128)} %get-tuple-element.22, f32[]{:T(128)} %get-tuple-element.21), channel_id=1, replica_groups=mesh['group'=8,'dev'=64] {'dev'}, use_global_device_ids=true, to_apply=%region_14.0 | all-reduce | flops 2 | bytes 16 | tf_op jit(solution)/shard_map/psum | solution.py:90
  1206.1 1.5 multiply_reduce_fusion.25
  1207.6 141.4 %psum.53 = f32[]{:T(128)} all-reduce(f32[]{:T(128)} %get-tuple-element.25), channel_id=1, replica_groups=mesh['group'=8,'dev'=64] {'dev'}, use_global_device_ids=true, to_apply=%region_25.27 | all-reduce | flops 1 | bytes 8 | tf_op jit(solution)/shard_map/psum | solution.py:90
  1350.3 0.9 multiply_add_fusion.1
  1351.2 31.6 %all_to_all.15 = f32[64,9,128]{2,1,0:T(8,128)S(1)} all-to-all(f32[64,9,128]{2,1,0:T(8,128)S(1)} %stack.28), channel_id=1, replica_groups=mesh['group'=8,'dev'=64] {'dev'}, dimensions={0} | all-to-all | bytes 589824 | tf_op jit(solution)/shard_map/all_to_all | solution.py:75
  1382.7 2.6 copy.46
  1385.4 16.3 gather_fusion.1
  1401.6 1.9 select_bitcast_fusion.1
  1403.6 0.6 copy.47
  1404.4 0.6 copy.54
  1405.0 24.5 %scatter_custom_fusion.2 = f32[9,8192]{0,1:T(8,128)} fusion(s32[4096]{0:T(1024)S(1)} %bitcast.57, f32[4096,9]{1,0:T(8,128)S(1)} %bitcast.51, f32[]{:T(128)} %constant.14.clone.1), kind=kCustom, calls=%fused_computation.9 | custom fusion | flops 36864 | bytes 294916 | tf_op jit(solution)/shard_map/vmap()/scatter-add | solution.py:62
  1429.5 3.5 copy.49
  1433.1 0.0 all-reduce.9.cloned.1.call-update
  1433.1 449.4 %all-reduce.9.cloned.1.call-done = f32[9,8192]{1,0:T(8,128)} async-done(((f32[9,8192]{1,0:T(8,128)}), f32[9,8192]{1,0:T(8,128)}) %all-reduce.9.cloned.1.call-update) | async-done | bytes 294928 | tf_op jit(solution)/shard_map/psum | solution.py:84
  1882.5 1.3 multiply_reduce_fusion.24
  1883.8 143.4 %psum.55 = f32[]{:T(128)} all-reduce(f32[]{:T(128)} %multiply_reduce_fusion.24), channel_id=1, replica_groups=mesh['group'=8,'dev'=64] {'dev'}, use_global_device_ids=true, to_apply=%region_34.36 | all-reduce | flops 1 | bytes 8 | tf_op jit(solution)/shard_map/psum | solution.py:90
  2028.5 1.4 multiply_subtract_fusion
  2029.9 0.0 copy-start.3
  2030.0 30.9 %all_to_all.16 = f32[64,9,128]{2,1,0:T(8,128)S(1)} all-to-all(f32[64,9,128]{2,1,0:T(8,128)S(1)} %stack.29), channel_id=1, replica_groups=mesh['group'=8,'dev'=64] {'dev'}, dimensions={0} | all-to-all | bytes 589824 | tf_op jit(solution)/shard_map/all_to_all | solution.py:75
  2060.8 2.6 copy.50
  2063.4 0.0 copy-done.3
  2063.4 16.3 gather_fusion.2
  2079.7 1.9 select_bitcast_fusion
  2081.7 0.6 copy.51
  2082.4 0.6 sub.133
  (25 shorter events, 0.6 us)
Async XLA Ops:
  7.2 507.3 %all-reduce.5.cloned.1.call-start = ((), (), s32[]{:S(2)}) async-start(), calls=%async_computation.3 | async-start | bytes 1572864 | tf_op jit(solution)/shard_map/psum | solution.py:84
  41.3 487.1 %copy-start.2 = (s32[8,512]{1,0:T(8,128)S(1)}, s32[8,512]{1,0:T(8,128)}, u32[]{:S(2)}) copy-start(s32[8,512]{1,0:T(8,128)} %param.9) | copy-start | bytes 49156
  516.1 44.2 %all-to-all-start = ((f32[64,9,128]{2,1,0:T(8,128)}), f32[64,9,128]{2,1,0:T(8,128)S(1)}, u32[]{:S(2)}, u32[]{:S(2)}) async-start(f32[64,9,128]{2,1,0:T(8,128)} %stack.27), calls=%async_computation | async-start | bytes 1048576 | tf_op jit(solution)/shard_map/all_to_all | solution.py:75
  528.3 533.6 %all-reduce.7.cloned.1.call-start = ((), (), s32[]{:S(2)}) async-start(), calls=%async_computation.4 | async-start | bytes 1048576 | tf_op jit(solution)/shard_map/psum | solution.py:84
  581.1 1.0 copy-start
  581.1 1.0 copy-start.1
  611.0 1271.5 %all-reduce.9.cloned.1.call-start = ((), (), s32[]{:S(2)}) async-start(), calls=%async_computation.5 | async-start | bytes 1048576 | tf_op jit(solution)/shard_map/psum | solution.py:84
  2029.9 33.5 %copy-start.3 = (f32[9,128]{1,0:T(8,128)}, f32[9,128]{1,0:T(8,128)S(1)}, u32[]{:S(2)}) copy-start(f32[9,128]{1,0:T(8,128)S(1)} %get-tuple-element.34) | copy-start | bytes 13828
Sparse Core Ops, SparseCore 0:
  41.4 472.9 all-reduce.4
  611.1 450.8 all-reduce.6
  1433.2 449.2 all-reduce.8
